TPU v7x, 32 devices: a whole 2x2x4 slice. The times are simulated.
32 devices in a mesh: blk: 8 (over z, y), gy: 4 (over x, core).
Axes of the slice: x: 2, y: 2, z: 4, core: 2. Of those that a mesh axis runs over, the one named last changes fastest.
Arguments:
- image: float32 [1, 2048, 2048], P(None, 'blk', 'gy'), may hold values from -6 to 6
- measured: float32 [1, 16, 2816], P(None, 'blk'), may hold values from -6 to 6
- row_weight: float32 [16, 2816], P('blk'), may hold values from 0.25 to 2
- col_weight: float32 [2048, 2048], P('blk', 'gy'), may hold values from 1 to 8
- band_weight: bfloat16 [16, 2048, 128], P('blk', 'gy'), may hold values from -0.01171875 to 0.01171875
- band_shift: int32 [16, 8], replicated, may hold values from 0 to 3
Outputs:
- updated: float32 [1, 2048, 2048], P(None, 'blk', 'gy')
Inputs may be any that keep to these rules, and one draw needn't show every extreme that they name: band_shift[t, s] is the number of panels by which slab s's footprint under tilt t starts beyond panel s * 2.
All inputs are finite; a program needn't handle non-finite values.
Results may differ from a plain program's by a relative error of at most 0.0025.
Values may be sent and summed in bfloat16 or wider, within the bound.
A program may use at most 64 MiB of HBM per device.

v0:
```python
import math
import jax
import jax.numpy as jnp
from jax import lax
from jax.sharding import PartitionSpec as P

PW = 128
SMOOTH = 0.25


def with_halo(cells, sides, width):
    for axis, dim in sides:
        count = lax.axis_size(axis)
        ends = count - 1
        head = lax.slice_in_dim(cells, 0, width, axis=dim)
        tail = lax.slice_in_dim(cells, cells.shape[dim] - width, cells.shape[dim], axis=dim)
        cells = jnp.concatenate(
            [
                lax.ppermute(tail, axis, [(i, (i + 1) % count) for i in range(ends)]),
                cells,
                lax.ppermute(head, axis, [((i + 1) % count, i) for i in range(ends)]),
            ],
            axis=dim,
        )
    return cells


def shift_rows(rows, direction):
    col_count = rows.shape[-2]
    bit_count = (col_count - 1).bit_length()
    column_index = jnp.arange(col_count, dtype=jnp.int32)[:, None]
    for level in range(bit_count):
        moved = jnp.roll(rows, direction * (1 << level), axis=-1)
        chosen = column_index >> level & 1 == 1
        rows = jnp.where(chosen, moved, rows)
    return rows


def diagonal_sum(product):
    leading = product.shape[:-2]
    col_count, band_width = product.shape[-2:]
    keep_pads = [(0, 0)] * (len(leading) + 1)
    padded = jnp.pad(product, keep_pads + [(0, col_count)])
    return jnp.sum(shift_rows(padded, 1), axis=-2)


def band_rows(panels, col_count, band_width):
    leading = panels.shape[:-1]
    window_len = panels.shape[-1]
    repeated = jnp.broadcast_to(panels[..., None, :], leading + (col_count, window_len))
    return shift_rows(repeated, -1)[..., :band_width]


def per_device(image, measured, row_weight, col_weight, band_weight, band_shift):
    row_count, col_count, depth_count = image.shape
    local_tilts = measured.shape[1]
    detector_len = measured.shape[2]
    band_width = band_weight.shape[2]
    window_len = col_count + band_width
    block_count = lax.axis_size("blk")
    myself = lax.axis_index("blk")
    tilt_count = local_tilts * block_count
    per_slab = col_count // PW
    zero_index = jnp.int32(0)
    copies = image.astype(jnp.bfloat16)
    slab_bins = ((jnp.arange(block_count, dtype=jnp.int32) * per_slab)[None, :] + band_shift) * PW
    first_tilt = myself * local_tilts
    own_bins = lax.dynamic_slice_in_dim(slab_bins, first_tilt, local_tilts, 0)
    group_size = math.gcd(tilt_count, 8)
    all_weights = lax.all_gather(band_weight, "blk", axis=0, tiled=True)
    weight_groups = all_weights.reshape(
        tilt_count // group_size, group_size, depth_count, band_width
    )

    def place_windows(running, windows, source):
        for tilt_slot in range(local_tilts):
            offset = own_bins[tilt_slot, source]
            corner = (zero_index, jnp.int32(tilt_slot), offset)
            current = lax.dynamic_slice(running, corner, (row_count, 1, window_len))
            running = lax.dynamic_update_slice(
                running, current + windows[tilt_slot][:, None, :], corner
            )
        return running

    initial = jnp.zeros((row_count, local_tilts, detector_len), jnp.float32)

    def project_group(weights):
        product = jnp.einsum("yiz,tzd->tyid", copies, weights, preferred_element_type=jnp.float32)
        return diagonal_sum(product)

    windows = lax.map(project_group, weight_groups)
    windows = windows.reshape(block_count, local_tilts, row_count, window_len)
    received = lax.all_to_all(windows, "blk", split_axis=0, concat_axis=0, tiled=True)

    def add_source(source, running):
        return place_windows(
            running, lax.dynamic_index_in_dim(received, source, 0, keepdims=False), source
        )

    partial_sum = lax.fori_loop(0, block_count, add_source, initial)
    projection = lax.psum(partial_sum, "gy")
    weighted = (row_weight[None] * (measured - projection)).astype(jnp.bfloat16)

    def cut_panels(slab_offsets):
        pieces = [
            lax.dynamic_slice(
                weighted[:, tilt_slot],
                (zero_index, slab_offsets[tilt_slot]),
                (row_count, window_len),
            )
            for tilt_slot in range(local_tilts)
        ]
        return jnp.stack(pieces, axis=1)

    outgoing = jax.vmap(cut_panels, in_axes=1, out_axes=1)(own_bins)
    arrived = lax.all_to_all(outgoing, "blk", split_axis=1, concat_axis=1, tiled=True)
    panels = arrived.reshape(row_count, tilt_count, window_len)
    panel_groups = panels.reshape(
        row_count, tilt_count // group_size, group_size, window_len
    ).transpose(1, 0, 2, 3)

    def back_group(running, operands):
        panel_part, weight_part = operands
        sheared = band_rows(panel_part, col_count, band_width)
        added = jnp.einsum(
            "ytid,tzd->yiz", sheared, weight_part, preferred_element_type=jnp.float32
        )
        return (running + added, None)

    start_back = jnp.zeros((row_count, col_count, depth_count), jnp.float32)
    backed, leftover = lax.scan(back_group, start_back, (panel_groups, weight_groups))
    padded_depth = with_halo(image.astype(jnp.bfloat16), (("gy", 2),), 1).astype(image.dtype)
    return (
        image
        + col_weight[None] * backed
        + SMOOTH * (padded_depth[:, :, :-2] + padded_depth[:, :, 2:] - 2.0 * image)
    )


def solution(mesh):
    return jax.shard_map(
        per_device,
        mesh=mesh,
        in_specs=(
            P(None, "blk", "gy"),
            P(None, "blk", None),
            P("blk", None),
            P("blk", "gy"),
            P("blk", "gy", None),
            P(),
        ),
        out_specs=P(None, "blk", "gy"),
        check_vma=False,
    )
```

profile of v0, /device:TPU:0, one launch (start us, length us, event | category | flops | bytes accessed | tf_op | source)
XLA Modules:
  0.0 203.8 jit_solution(14922307778124006677)
XLA Ops:
  7.3 1.1 convert_element_type.22
  9.0 3.0 %collective-permute-start = (bf16[1,256,1]{2,1,0:T(8,128)(2,1)}, bf16[1,256,1]{2,1,0:T(8,128)(2,1)}, u32[]{:S(2)}, u32[]{:S(2)}) collective-permute-start(bf16[1,256,1]{2,1,0:T(8,128)(2,1)} %get-tuple-element.283), channel_id=1, source_target_pairs={{0,1},{1,2},{2,3},{4,5},{5,6},{6,7},{8,9},{9,10},{10,11},{12,13},{... | collective-permute-start | bytes 1544 | tf_op jit(solution)/shard_map/ppermute | solution.py:19
  12.0 1.3 collective-permute-start.1
  15.5 46.0 %all-gather.2.cloned.1.call-done = bf16[16,512,128]{2,1,0:T(8,128)(2,1)} async-done(((bf16[2,512,128]{2,1,0:T(8,128)(2,1)}), bf16[16,512,128]{2,1,0:T(8,128)(2,1)}) %all-gather.2.cloned.1.call-update) | async-done | bytes 2097168 | tf_op jit(solution)/shard_map/all_gather | solution.py:70
  61.5 14.9 %while.38 = (s32[]{:T(128)}, f32[2,8,1,384]{3,2,1,0:T(1,128)}, bf16[2,8,512,128]{3,2,1,0:T(8,128)(2,1)}, bf16[1,256,512]{2,1,0:T(8,128)(2,1)S(1)}, s32[]{:T(128)}) while((s32[]{:T(128)}, f32[2,8,1,384]{3,2,1,0:T(1,128)}, bf16[2,8,512,128]{3,2,1,0:T(8,128)(2,1)}, bf16[1,256,512]{2,1,0:T(8,128)(2,1)S(1)}, s32[]{:T(128)}) %tuple.126), condition=%wide.region_2.3_spmd, body=%wide.region_0.2_spmd.sunk | while | flops 281021440 | bytes 108389440 | solution.py:91
  61.5 1.7 convolution_bitcast_fusion.3
  69.0 1.7 convolution_bitcast_fusion.3
  76.4 3.3 %all-to-all-start = ((f32[8,2,1,384]{3,2,1,0:T(1,128)}), f32[8,2,1,384]{3,2,1,0:T(1,128)S(1)}, u32[]{:S(2)}, u32[]{:S(2)}) async-start(f32[8,2,1,384]{3,2,1,0:T(1,128)} %bitcast.12), calls=%async_computation | async-start | bytes 49152 | tf_op jit(solution)/shard_map/all_to_all | solution.py:93
  79.9 6.4 %all-to-all-done = f32[8,2,1,384]{3,2,1,0:T(1,128)S(1)} async-done(((f32[8,2,1,384]{3,2,1,0:T(1,128)}), f32[8,2,1,384]{3,2,1,0:T(1,128)S(1)}, u32[]{:S(2)}, u32[]{:S(2)}) %all-to-all-start) | async-done | bytes 24608 | tf_op jit(solution)/shard_map/all_to_all | solution.py:93
  86.3 35.3 %while.39 = (s32[]{:T(128)}, f32[1,2,2816]{2,1,0:T(2,128)S(1)}, s32[2,8]{1,0:T(2,128)S(1)}, f32[8,2,1,384]{3,2,1,0:T(1,128)S(1)}, s32[]{:T(128)}, /*index=5*/s32[]{:T(128)}, s32[]{:T(128)}, s32[]{}) while((s32[]{:T(128)}, f32[1,2,2816]{2,1,0:T(2,128)S(1)}, s32[2,8]{1,0:T(2,128)S(1)}, f32[8,2,1,384]{3,2,1,0:T(1,128)S(1)}, s32[]{:T(128)}, ...), condition=%wide.region_4.5_spmd, body=%wide.region_3.4_spmd.sunk | while | flops 777 | bytes 15573 | solution.py:100
  121.7 10.3 %psum.7 = f32[1,2,2816]{2,1,0:T(2,128)S(1)} all-reduce(f32[1,2,2816]{2,1,0:T(2,128)S(1)} %get-tuple-element.160), channel_id=1, replica_groups=mesh['blk'=8,'gy'=4] {'gy'}, use_global_device_ids=true, to_apply=%region_5.6 | all-reduce | flops 5632 | bytes 45056 | tf_op jit(solution)/shard_map/psum | solution.py:101
  132.0 11.8 %while.40 = (s32[]{:T(128)}, bf16[1,2816]{1,0:T(2,128)(2,1)S(1)}, s32[8,2]{0,1:T(2,128)S(1)}, bf16[8,1,384]{2,0,1:T(8,128)(2,1)S(1)}, s32[]{:T(128)}, /*index=5*/s32[]{:T(128)}) while((s32[]{:T(128)}, bf16[1,2816]{1,0:T(2,128)(2,1)S(1)}, s32[8,2]{0,1:T(2,128)S(1)}, bf16[8,1,384]{2,0,1:T(8,128)(2,1)S(1)}, s32[]{:T(128)}, /*index=5*/s32[]{:T(128)}) %tuple.118), condition=%wide.while_cond, body=%wide.while_body.sunk | while | flops 2 | bytes 3177 | solution.py:106
  132.7 0.8 dynamic-slice_bitcast_fusion.6
  134.2 0.8 dynamic-slice_bitcast_fusion.6
  135.7 0.8 dynamic-slice_bitcast_fusion.6
  137.2 0.8 dynamic-slice_bitcast_fusion.6
  138.6 0.8 dynamic-slice_bitcast_fusion.6
  140.1 0.8 dynamic-slice_bitcast_fusion.6
  141.6 0.8 dynamic-slice_bitcast_fusion.6
  143.1 0.8 dynamic-slice_bitcast_fusion.6
  143.9 10.7 %while.41 = (s32[]{:T(128)}, bf16[1,2816]{1,0:T(2,128)(2,1)S(1)}, s32[8,2]{0,1:T(2,128)S(1)}, bf16[8,1,384]{2,0,1:T(8,128)(2,1)S(1)}, s32[]{:T(128)}, /*index=5*/s32[]{:T(128)}) while((s32[]{:T(128)}, bf16[1,2816]{1,0:T(2,128)(2,1)S(1)}, s32[8,2]{0,1:T(2,128)S(1)}, bf16[8,1,384]{2,0,1:T(8,128)(2,1)S(1)}, s32[]{:T(128)}, /*index=5*/s32[]{:T(128)}) %tuple.115), condition=%wide.while_cond.1, body=%wide.while_body.1.sunk | while | flops 2 | bytes 3177 | solution.py:106
  155.2 3.5 %all-to-all-start.1 = ((bf16[1,8,2,384]{3,2,0,1:T(2,128)(2,1)}), bf16[1,8,2,384]{3,2,0,1:T(2,128)(2,1)S(1)}, u32[]{:S(2)}, u32[]{:S(2)}) async-start(bf16[1,8,2,384]{3,2,0,1:T(2,128)(2,1)} %copy.33), calls=%async_computation.1 | async-start | bytes 24576 | tf_op jit(solution)/shard_map/all_to_all | solution.py:116
  158.7 1.9 maximum_convert_fusion
  160.6 4.4 %all-to-all-done.1 = bf16[1,8,2,384]{3,2,0,1:T(2,128)(2,1)S(1)} async-done(((bf16[1,8,2,384]{3,2,0,1:T(2,128)(2,1)}), bf16[1,8,2,384]{3,2,0,1:T(2,128)(2,1)S(1)}, u32[]{:S(2)}, u32[]{:S(2)}) %all-to-all-start.1) | async-done | bytes 12320 | tf_op jit(solution)/shard_map/all_to_all | solution.py:116
  165.0 29.1 %while.42 = (s32[]{:T(128)}, f32[1,256,512]{2,1,0:T(8,128)}, bf16[2,1,8,384]{3,2,0,1:T(8,128)(2,1)S(1)}, bf16[2,8,512,128]{3,2,1,0:T(8,128)(2,1)}, s32[]{:T(128)}, /*index=5*/s32[]{:T(128)}) while((s32[]{:T(128)}, f32[1,256,512]{2,1,0:T(8,128)}, bf16[2,1,8,384]{3,2,0,1:T(8,128)(2,1)S(1)}, bf16[2,8,512,128]{3,2,1,0:T(8,128)(2,1)}, ...), condition=%wide.region_7.8_spmd.clone, body=%wide.region_6.7_spmd.clone.sunk | while | flops 301471744 | bytes 67193432 | solution.py:131
  167.1 1.1 maximum_select_fusion.34
  176.3 0.9 slice.383
  177.2 2.3 %fusion.41 = f32[1,256,512]{2,1,0:T(8,128)} fusion(bf16[2,8,512,128]{3,2,1,0:T(8,128)(2,1)S(1)} %copy-done, s32[]{:T(128)} %get-tuple-element.503, bf16[1,8,256,128]{3,2,1,0:T(8,128)(2,1)} %slice.383, bf16[1,8,256,256]{3,2,1,0:T(8,128)(2,1)S(1)} %slice.384, f32[1,256,512]{2,1,0:T(8,128)} %get-tuple-element.504, ...), kind=kOutput, calls=%fused_computation.42.clone.1 | convolution fusion | flops 270008320 | bytes 3670533 | tf_op jit(solution)/shard_map/while/body/eval_jaxpr/ytid,tzd->yiz/dot_general | solution.py:125
  181.6 1.1 maximum_select_fusion.34
  190.8 0.9 slice.383
  191.7 2.5 %fusion.41 = f32[1,256,512]{2,1,0:T(8,128)} fusion(bf16[2,8,512,128]{3,2,1,0:T(8,128)(2,1)S(1)} %copy-done, s32[]{:T(128)} %get-tuple-element.503, bf16[1,8,256,128]{3,2,1,0:T(8,128)(2,1)} %slice.383, bf16[1,8,256,256]{3,2,1,0:T(8,128)(2,1)S(1)} %slice.384, f32[1,256,512]{2,1,0:T(8,128)} %get-tuple-element.504, ...), kind=kOutput, calls=%fused_computation.42.clone.1 | convolution fusion | flops 270008320 | bytes 3670533 | tf_op jit(solution)/shard_map/while/body/eval_jaxpr/ytid,tzd->yiz/dot_general | solution.py:125
  194.2 2.8 %fusion.19 = f32[1,256,512]{2,1,0:T(8,128)} fusion(f32[1,256,514]{2,1,0:T(8,128)} %maximum_convert_fusion, f32[1,256,512]{2,1,0:T(8,128)} %param.12, f32[1,256,512]{2,1,0:T(8,128)} %get-tuple-element.161, f32[256,512]{1,0:T(8,128)} %param.15), kind=kLoop, calls=%fused_computation.65 | loop fusion | flops 917504 | bytes 3145728 | tf_op jit(solution)/shard_map/add | solution.py:134
  (263 shorter events, 59.6 us)
Async XLA Ops:
  6.5 55.0 %all-gather.2.cloned.1.call-start = ((), (), s32[]{:S(2)}) async-start(), calls=%async_computation.2 | async-start | bytes 2359296 | tf_op jit(solution)/shard_map/all_gather | solution.py:70
  9.0 149.7 %collective-permute-start = (bf16[1,256,1]{2,1,0:T(8,128)(2,1)}, bf16[1,256,1]{2,1,0:T(8,128)(2,1)}, u32[]{:S(2)}, u32[]{:S(2)}) collective-permute-start(bf16[1,256,1]{2,1,0:T(8,128)(2,1)} %get-tuple-element.283), channel_id=1, source_target_pairs={{0,1},{1,2},{2,3},{4,5},{5,6},{6,7},{8,9},{9,10},{10,11},{12,13},{... | collective-permute-start | bytes 1544 | tf_op jit(solution)/shard_map/ppermute | solution.py:19
  12.0 146.7 %collective-permute-start.1 = (bf16[1,256,1]{2,1,0:T(8,128)(2,1)}, bf16[1,256,1]{2,1,0:T(8,128)(2,1)}, u32[]{:S(2)}, u32[]{:S(2)}) collective-permute-start(bf16[1,256,1]{2,1,0:T(8,128)(2,1)} %get-tuple-element.284), channel_id=1, source_target_pairs={{1,0},{2,1},{3,2},{5,4},{6,5},{7,6},{9,8},{10,9},{11,10},{13,12},{... | collective-permute-start | bytes 1544 | tf_op jit(solution)/shard_map/ppermute | solution.py:21
  14.2 0.6 copy-start.1
  61.5 18.3 %copy-start.5 = (s32[8]{0:T(128)S(1)}, s32[8]{0:T(128)}, u32[]{:S(2)}) copy-start(s32[8]{0:T(128)} %get-tuple-element.237) | copy-start | bytes 100
  61.5 18.3 %copy-start.6 = (s32[8]{0:T(128)S(1)}, s32[8]{0:T(128)}, u32[]{:S(2)}) copy-start(s32[8]{0:T(128)} %get-tuple-element.238) | copy-start | bytes 100
  61.5 18.3 %copy-start.2 = (s32[2,8]{0,1:T(8,128)S(1)}, s32[2,8]{0,1:T(8,128)}, u32[]{:S(2)}) copy-start(s32[2,8]{0,1:T(8,128)} %copy-done.1) | copy-start | bytes 196
  61.5 70.4 %copy-start.3 = (f32[2,2816]{1,0:T(2,128)S(1)}, f32[2,2816]{1,0:T(2,128)}, u32[]{:S(2)}) copy-start(f32[2,2816]{1,0:T(2,128)} %param.14) | copy-start | bytes 67588
  61.5 70.4 %copy-start.4 = (f32[1,2,2816]{2,1,0:T(2,128)S(1)}, f32[1,2,2816]{2,1,0:T(2,128)}, u32[]{:S(2)}) copy-start(f32[1,2,2816]{2,1,0:T(2,128)} %param.13) | copy-start | bytes 67588
  76.4 9.9 %all-to-all-start = ((f32[8,2,1,384]{3,2,1,0:T(1,128)}), f32[8,2,1,384]{3,2,1,0:T(1,128)S(1)}, u32[]{:S(2)}, u32[]{:S(2)}) async-start(f32[8,2,1,384]{3,2,1,0:T(1,128)} %bitcast.12), calls=%async_computation | async-start | bytes 49152 | tf_op jit(solution)/shard_map/all_to_all | solution.py:93
  155.2 9.8 %all-to-all-start.1 = ((bf16[1,8,2,384]{3,2,0,1:T(2,128)(2,1)}), bf16[1,8,2,384]{3,2,0,1:T(2,128)(2,1)S(1)}, u32[]{:S(2)}, u32[]{:S(2)}) async-start(bf16[1,8,2,384]{3,2,0,1:T(2,128)(2,1)} %copy.33), calls=%async_computation.1 | async-start | bytes 24576 | tf_op jit(solution)/shard_map/all_to_all | solution.py:116
  175.5 1.7 copy-start
  190.0 1.7 copy-start
Sparse Core Ops, SparseCore 0:
  9.5 51.9 all-gather.1
where the time goes:
time: 205 us; the launch traced here: 204 us
  waiting for transfers between devices  57.6 us (28%)
  local copies, waits for them, and re-layouts  49.3 us (24%)
  loops' own time  28.2 us (14%)
  other arithmetic  25.6 us (12%)
  between operations  13.6 us (7%)
  starting transfers between devices  11.1 us (5%)
  blocking collectives  10.3 us (5%)
  matrix products  8.25 us (4%)
    all_gather x1, waiting for transfers between devices, per_device(): all_weights = lax.all_gather(band_weight, 'blk', axis=0, tiled=True)  46 us
    another operation x1, loops' own time, per_device(): partial_sum = lax.fori_loop(0, block_count, add_source, initial)  27.2 us
    gather x64, local copies, waits for them, and re-layouts  22.3 us
    select_n x28, other arithmetic, shift_rows(): rows = jnp.where(chosen, moved, rows)  16.4 us
    slice x60, local copies, waits for them, and re-layouts, shift_rows(): moved = jnp.roll(rows, direction * (1 << level), axis=-1)  15.1 us
    psum x1, blocking collectives, per_device(): projection = lax.psum(partial_sum, 'gy')  10.3 us
    all_to_all x1, waiting for transfers between devices, per_device(): lax.all_to_all(windows, 'blk', split_axis=0, concat_axis=0, tiled=True)  6.42 us
    dot_general x2, matrix products, back_group(): jnp.einsum('ytid,tzd->yiz', sheared, weight_part, preferred_element_type=...  4.81 us
  transfers between devices with their start and end apart: 5, of which 3 were waited for; matrix products, arithmetic and copies ran while one was open for 25% of the time, Pallas kernels for 0%

commit v1 on v0

--- a/solution.py
+++ b/solution.py
@@ -113,7 +113,10 @@
         return jnp.stack(pieces, axis=1)
 
     outgoing = jax.vmap(cut_panels, in_axes=1, out_axes=1)(own_bins)
-    arrived = lax.all_to_all(outgoing, "blk", split_axis=1, concat_axis=1, tiled=True)
+    arrived = jnp.concatenate(
+        lax.all_to_all(jnp.stack(jnp.split(outgoing, lax.axis_size("blk"), axis=1)), "blk", 0, 0),
+        axis=1,
+    )
     panels = arrived.reshape(row_count, tilt_count, window_len)
     panel_groups = panels.reshape(
         row_count, tilt_count // group_size, group_size, window_len

time: 205 us -> 211 us (1.029)
  local copies, waits for them, and re-layouts: 49.3 us -> 53.3 us
  loops' own time: 28.2 us -> 30.5 us
    unnamed x14 -> x21, local copies, waits for them, and re-layouts: 0.62 us -> 4.58 us
    another operation x1, loops' own time: 27.2 us -> 29.5 us  [per_device(): partial_sum = lax.fori_loop(0, block_count, add_source, initial)]
  transfers between devices with their start and end apart: 5 -> 5, of which waited for: 3 -> 3; matrix products, arithmetic and copies ran while one was open for 25% -> 26% of each run, Pallas kernels for 0% -> 0%
where the time goes in v1:
time: 211 us; the launch traced here: 210 us
  waiting for transfers between devices  57.5 us (27%)
  local copies, waits for them, and re-layouts  53.3 us (25%)
  loops' own time  30.5 us (14%)
  other arithmetic  25.6 us (12%)
  between operations  13.6 us (6%)
  starting transfers between devices  11.1 us (5%)
  blocking collectives  10.3 us (5%)
  matrix products  8.26 us (4%)
    all_gather x1, waiting for transfers between devices, per_device(): all_weights = lax.all_gather(band_weight, 'blk', axis=0, tiled=True)  46 us
    another operation x1, loops' own time, per_device(): partial_sum = lax.fori_loop(0, block_count, add_source, initial)  29.5 us
    gather x64, local copies, waits for them, and re-layouts  21.9 us
    select_n x28, other arithmetic, shift_rows(): rows = jnp.where(chosen, moved, rows)  16.4 us
    slice x60, local copies, waits for them, and re-layouts, shift_rows(): moved = jnp.roll(rows, direction * (1 << level), axis=-1)  15.1 us
    psum x1, blocking collectives, per_device(): projection = lax.psum(partial_sum, 'gy')  10.3 us
    all_to_all x1, waiting for transfers between devices, per_device(): lax.all_to_all(windows, 'blk', split_axis=0, concat_axis=0, tiled=True)  6.42 us
    dynamic_slice x8, local copies, waits for them, and re-layouts, place_windows(): offset = own_bins[tilt_slot, source]  5.2 us
  transfers between devices with their start and end apart: 5, of which 3 were waited for; matrix products, arithmetic and copies ran while one was open for 26% of the time, Pallas kernels for 0%

profile of v1, /device:TPU:0, one launch (start us, length us, event | category | flops | bytes accessed | tf_op | source)
XLA Modules:
  0.0 210.1 jit_solution(7843924293539976151)
XLA Ops:
  7.3 1.1 convert_element_type.22
  9.0 3.0 %collective-permute-start = (bf16[1,256,1]{2,1,0:T(8,128)(2,1)}, bf16[1,256,1]{2,1,0:T(8,128)(2,1)}, u32[]{:S(2)}, u32[]{:S(2)}) collective-permute-start(bf16[1,256,1]{2,1,0:T(8,128)(2,1)} %get-tuple-element.339), channel_id=1, source_target_pairs={{0,1},{1,2},{2,3},{4,5},{5,6},{6,7},{8,9},{9,10},{10,11},{12,13},{... | collective-permute-start | bytes 1544 | tf_op jit(solution)/shard_map/ppermute | solution.py:19
  12.0 1.3 collective-permute-start.1
  15.5 46.0 %all-gather.2.cloned.1.call-done = bf16[16,512,128]{2,1,0:T(8,128)(2,1)} async-done(((bf16[2,512,128]{2,1,0:T(8,128)(2,1)}), bf16[16,512,128]{2,1,0:T(8,128)(2,1)}) %all-gather.2.cloned.1.call-update) | async-done | bytes 2097168 | tf_op jit(solution)/shard_map/all_gather | solution.py:70
  61.5 14.9 %while.38 = (s32[]{:T(128)}, f32[2,8,1,384]{3,2,1,0:T(1,128)}, bf16[2,8,512,128]{3,2,1,0:T(8,128)(2,1)}, bf16[1,256,512]{2,1,0:T(8,128)(2,1)S(1)}, s32[]{:T(128)}) while((s32[]{:T(128)}, f32[2,8,1,384]{3,2,1,0:T(1,128)}, bf16[2,8,512,128]{3,2,1,0:T(8,128)(2,1)}, bf16[1,256,512]{2,1,0:T(8,128)(2,1)S(1)}, s32[]{:T(128)}) %tuple.147), condition=%wide.region_2.3_spmd, body=%wide.region_0.2_spmd.sunk | while | flops 281021440 | bytes 108389440 | solution.py:91
  61.5 1.7 convolution_bitcast_fusion.3
  69.0 1.7 convolution_bitcast_fusion.3
  76.4 3.3 %all-to-all-start = ((f32[8,2,1,384]{3,2,1,0:T(1,128)}), f32[8,2,1,384]{3,2,1,0:T(1,128)S(1)}, u32[]{:S(2)}, u32[]{:S(2)}) async-start(f32[8,2,1,384]{3,2,1,0:T(1,128)} %bitcast.12), calls=%async_computation | async-start | bytes 49152 | tf_op jit(solution)/shard_map/all_to_all | solution.py:93
  79.9 6.4 %all-to-all-done = f32[8,2,1,384]{3,2,1,0:T(1,128)S(1)} async-done(((f32[8,2,1,384]{3,2,1,0:T(1,128)}), f32[8,2,1,384]{3,2,1,0:T(1,128)S(1)}, u32[]{:S(2)}, u32[]{:S(2)}) %all-to-all-start) | async-done | bytes 24608 | tf_op jit(solution)/shard_map/all_to_all | solution.py:93
  86.3 38.1 %while.39 = (s32[]{:T(128)}, f32[1,2,2816]{2,1,0:T(2,128)S(1)}, s32[2,8]{1,0:T(2,128)S(1)}, f32[8,2,1,384]{3,2,1,0:T(1,128)S(1)}, s32[]{:T(128)}, /*index=5*/s32[]{:T(128)}, s32[]{:T(128)}, s32[]{}) while((s32[]{:T(128)}, f32[1,2,2816]{2,1,0:T(2,128)S(1)}, s32[2,8]{1,0:T(2,128)S(1)}, f32[8,2,1,384]{3,2,1,0:T(1,128)S(1)}, s32[]{:T(128)}, ...), condition=%wide.region_4.5_spmd, body=%wide.region_3.4_spmd.sunk | while | flops 777 | bytes 15573 | solution.py:100
  124.5 10.3 %psum.7 = f32[1,2,2816]{2,1,0:T(2,128)S(1)} all-reduce(f32[1,2,2816]{2,1,0:T(2,128)S(1)} %get-tuple-element.160), channel_id=1, replica_groups=mesh['blk'=8,'gy'=4] {'gy'}, use_global_device_ids=true, to_apply=%region_5.6 | all-reduce | flops 5632 | bytes 45056 | tf_op jit(solution)/shard_map/psum | solution.py:101
  134.8 10.3 %while.40 = (s32[]{:T(128)}, bf16[1,2816]{1,0:T(2,128)(2,1)S(1)}, s32[8,2]{0,1:T(2,128)S(1)}, bf16[8,1,384]{2,0,1:T(8,128)(2,1)S(1)}, s32[]{:T(128)}, /*index=5*/s32[]{:T(128)}) while((s32[]{:T(128)}, bf16[1,2816]{1,0:T(2,128)(2,1)S(1)}, s32[8,2]{0,1:T(2,128)S(1)}, bf16[8,1,384]{2,0,1:T(8,128)(2,1)S(1)}, s32[]{:T(128)}, /*index=5*/s32[]{:T(128)}) %tuple.139), condition=%wide.while_cond, body=%wide.while_body.sunk | while | flops 2 | bytes 3177 | solution.py:106
  145.1 11.8 %while.41 = (s32[]{:T(128)}, bf16[1,2816]{1,0:T(2,128)(2,1)S(1)}, s32[8,2]{0,1:T(2,128)S(1)}, bf16[8,1,384]{2,0,1:T(8,128)(2,1)S(1)}, s32[]{:T(128)}, /*index=5*/s32[]{:T(128)}) while((s32[]{:T(128)}, bf16[1,2816]{1,0:T(2,128)(2,1)S(1)}, s32[8,2]{0,1:T(2,128)S(1)}, bf16[8,1,384]{2,0,1:T(8,128)(2,1)S(1)}, s32[]{:T(128)}, /*index=5*/s32[]{:T(128)}) %tuple.136), condition=%wide.while_cond.1, body=%wide.while_body.1.sunk | while | flops 2 | bytes 3177 | solution.py:106
  145.8 0.8 dynamic-slice_bitcast_fusion.7
  147.3 0.8 dynamic-slice_bitcast_fusion.7
  148.7 0.8 dynamic-slice_bitcast_fusion.7
  150.2 0.8 dynamic-slice_bitcast_fusion.7
  151.7 0.8 dynamic-slice_bitcast_fusion.7
  153.2 0.8 dynamic-slice_bitcast_fusion.7
  154.7 0.8 dynamic-slice_bitcast_fusion.7
  156.1 0.8 dynamic-slice_bitcast_fusion.7
  161.5 3.5 %all-to-all-start.1 = ((bf16[8,1,1,2,384]{4,3,2,1,0:T(2,128)(2,1)}), bf16[8,1,1,2,384]{4,3,2,1,0:T(2,128)(2,1)S(1)}, u32[]{:S(2)}, u32[]{:S(2)}) async-start(bf16[8,1,1,2,384]{4,3,2,1,0:T(2,128)(2,1)} %constant_dynamic-update-slice_fusion), calls=%async_computation.1 | async-start | bytes 24576 | tf_op jit(solution)/shard_map/all_to_all | solution.py:117
  165.0 1.9 maximum_convert_fusion
  166.9 4.4 %all-to-all-done.1 = bf16[8,1,1,2,384]{4,3,2,1,0:T(2,128)(2,1)S(1)} async-done(((bf16[8,1,1,2,384]{4,3,2,1,0:T(2,128)(2,1)}), bf16[8,1,1,2,384]{4,3,2,1,0:T(2,128)(2,1)S(1)}, u32[]{:S(2)}, u32[]{:S(2)}) %all-to-all-start.1) | async-done | bytes 12320 | tf_op jit(solution)/shard_map/all_to_all | solution.py:117
  171.3 29.2 %while.42 = (s32[]{:T(128)}, f32[1,256,512]{2,1,0:T(8,128)}, bf16[2,1,8,384]{3,2,0,1:T(8,128)(2,1)S(1)}, bf16[2,8,512,128]{3,2,1,0:T(8,128)(2,1)}, s32[]{:T(128)}, /*index=5*/s32[]{:T(128)}) while((s32[]{:T(128)}, f32[1,256,512]{2,1,0:T(8,128)}, bf16[2,1,8,384]{3,2,0,1:T(8,128)(2,1)S(1)}, bf16[2,8,512,128]{3,2,1,0:T(8,128)(2,1)}, ...), condition=%wide.region_7.8_spmd.clone, body=%wide.region_6.7_spmd.clone.sunk | while | flops 301471744 | bytes 67193432 | solution.py:134
  173.4 1.1 maximum_select_fusion.34
  182.6 0.9 slice.383
  183.5 2.3 %fusion.42 = f32[1,256,512]{2,1,0:T(8,128)} fusion(bf16[2,8,512,128]{3,2,1,0:T(8,128)(2,1)S(1)} %copy-done, s32[]{:T(128)} %get-tuple-element.567, bf16[1,8,256,128]{3,2,1,0:T(8,128)(2,1)} %slice.383, bf16[1,8,256,256]{3,2,1,0:T(8,128)(2,1)S(1)} %slice.384, f32[1,256,512]{2,1,0:T(8,128)} %get-tuple-element.568, ...), kind=kOutput, calls=%fused_computation.42.clone.1 | convolution fusion | flops 270008320 | bytes 3670533 | tf_op jit(solution)/shard_map/while/body/eval_jaxpr/ytid,tzd->yiz/dot_general | solution.py:128
  187.9 1.1 maximum_select_fusion.34
  197.1 0.9 slice.383
  198.0 2.5 %fusion.42 = f32[1,256,512]{2,1,0:T(8,128)} fusion(bf16[2,8,512,128]{3,2,1,0:T(8,128)(2,1)S(1)} %copy-done, s32[]{:T(128)} %get-tuple-element.567, bf16[1,8,256,128]{3,2,1,0:T(8,128)(2,1)} %slice.383, bf16[1,8,256,256]{3,2,1,0:T(8,128)(2,1)S(1)} %slice.384, f32[1,256,512]{2,1,0:T(8,128)} %get-tuple-element.568, ...), kind=kOutput, calls=%fused_computation.42.clone.1 | convolution fusion | flops 270008320 | bytes 3670533 | tf_op jit(solution)/shard_map/while/body/eval_jaxpr/ytid,tzd->yiz/dot_general | solution.py:128
  200.5 2.8 %fusion.19 = f32[1,256,512]{2,1,0:T(8,128)} fusion(f32[1,256,514]{2,1,0:T(8,128)} %maximum_convert_fusion, f32[1,256,512]{2,1,0:T(8,128)} %param.12, f32[1,256,512]{2,1,0:T(8,128)} %get-tuple-element.161, f32[256,512]{1,0:T(8,128)} %param.15), kind=kLoop, calls=%fused_computation.65 | loop fusion | flops 917504 | bytes 3145728 | tf_op jit(solution)/shard_map/add | solution.py:137
  (271 shorter events, 63.6 us)
Async XLA Ops:
  6.5 55.0 %all-gather.2.cloned.1.call-start = ((), (), s32[]{:S(2)}) async-start(), calls=%async_computation.2 | async-start | bytes 2359296 | tf_op jit(solution)/shard_map/all_gather | solution.py:70
  9.0 155.9 %collective-permute-start = (bf16[1,256,1]{2,1,0:T(8,128)(2,1)}, bf16[1,256,1]{2,1,0:T(8,128)(2,1)}, u32[]{:S(2)}, u32[]{:S(2)}) collective-permute-start(bf16[1,256,1]{2,1,0:T(8,128)(2,1)} %get-tuple-element.339), channel_id=1, source_target_pairs={{0,1},{1,2},{2,3},{4,5},{5,6},{6,7},{8,9},{9,10},{10,11},{12,13},{... | collective-permute-start | bytes 1544 | tf_op jit(solution)/shard_map/ppermute | solution.py:19
  12.0 153.0 %collective-permute-start.1 = (bf16[1,256,1]{2,1,0:T(8,128)(2,1)}, bf16[1,256,1]{2,1,0:T(8,128)(2,1)}, u32[]{:S(2)}, u32[]{:S(2)}) collective-permute-start(bf16[1,256,1]{2,1,0:T(8,128)(2,1)} %get-tuple-element.340), channel_id=1, source_target_pairs={{1,0},{2,1},{3,2},{5,4},{6,5},{7,6},{9,8},{10,9},{11,10},{13,12},{... | collective-permute-start | bytes 1544 | tf_op jit(solution)/shard_map/ppermute | solution.py:21
  14.2 0.6 copy-start.1
  61.5 18.3 %copy-start.5 = (s32[8]{0:T(128)S(1)}, s32[8]{0:T(128)}, u32[]{:S(2)}) copy-start(s32[8]{0:T(128)} %get-tuple-element.293) | copy-start | bytes 100
  61.5 18.3 %copy-start.6 = (s32[8]{0:T(128)S(1)}, s32[8]{0:T(128)}, u32[]{:S(2)}) copy-start(s32[8]{0:T(128)} %get-tuple-element.294) | copy-start | bytes 100
  61.5 18.3 %copy-start.2 = (s32[2,8]{0,1:T(8,128)S(1)}, s32[2,8]{0,1:T(8,128)}, u32[]{:S(2)}) copy-start(s32[2,8]{0,1:T(8,128)} %copy-done.1) | copy-start | bytes 196
  61.5 73.2 %copy-start.3 = (f32[2,2816]{1,0:T(2,128)S(1)}, f32[2,2816]{1,0:T(2,128)}, u32[]{:S(2)}) copy-start(f32[2,2816]{1,0:T(2,128)} %param.14) | copy-start | bytes 67588
  61.5 73.2 %copy-start.4 = (f32[1,2,2816]{2,1,0:T(2,128)S(1)}, f32[1,2,2816]{2,1,0:T(2,128)}, u32[]{:S(2)}) copy-start(f32[1,2,2816]{2,1,0:T(2,128)} %param.13) | copy-start | bytes 67588
  76.4 9.9 %all-to-all-start = ((f32[8,2,1,384]{3,2,1,0:T(1,128)}), f32[8,2,1,384]{3,2,1,0:T(1,128)S(1)}, u32[]{:S(2)}, u32[]{:S(2)}) async-start(f32[8,2,1,384]{3,2,1,0:T(1,128)} %bitcast.12), calls=%async_computation | async-start | bytes 49152 | tf_op jit(solution)/shard_map/all_to_all | solution.py:93
  161.5 9.8 %all-to-all-start.1 = ((bf16[8,1,1,2,384]{4,3,2,1,0:T(2,128)(2,1)}), bf16[8,1,1,2,384]{4,3,2,1,0:T(2,128)(2,1)S(1)}, u32[]{:S(2)}, u32[]{:S(2)}) async-start(bf16[8,1,1,2,384]{4,3,2,1,0:T(2,128)(2,1)} %constant_dynamic-update-slice_fusion), calls=%async_computation.1 | async-start | bytes 24576 | tf_op jit(solution)/shard_map/all_to_all | solution.py:117
  181.7 1.7 copy-start
  196.3 1.7 copy-start
Sparse Core Ops, SparseCore 0:
  9.5 51.9 all-gather.1
